TPU v7x, 256 devices: a whole 4x4x8 slice. The times are simulated.
256 devices in a mesh: dp: 32 (over y, z), expert: 8 (over x, core).
Axes of the slice: x: 4, y: 4, z: 8, core: 2. Of those that a mesh axis runs over, the one named last changes fastest.
Arguments:
- tokens: bfloat16 [2048, 3072], P('expert'), may hold values from -6 to 6
- cotangent: bfloat16 [2048, 3072], P('expert'), may hold values from -6 to 6
- routes: int32 [2048, 2], P('expert'), may hold values from 0 to 7, all different within a row; in each aligned block of 256 rows (0 to 255, 256 to 511, ...) at most 128 rows name the same one
- gate_values: bfloat16 [2048, 2], P('expert'), may hold values from 0.049804688 to 0.94921875
- gate_weight: bfloat16 [8, 3072, 8192], P('expert', None, 'dp'), may hold values from -0.109375 to 0.109375
- up_weight: bfloat16 [8, 3072, 8192], P('expert', None, 'dp'), may hold values from -0.109375 to 0.109375
- down_weight: bfloat16 [8, 3072, 8192], P('expert', None, 'dp'), may hold values from -0.0625 to 0.0625
Outputs:
- clipped: bfloat16 [8, 3, 3072, 8192], P('expert', None, 'dp')
- d_tokens: bfloat16 [3072, 2048], P('dp', 'expert')
Inputs may be any that keep to these rules, and one draw needn't show every extreme that they name: `routes`: each row names two different experts. Within the 256 rows of one device along expert (aligned blocks), no expert is named by more than 128 rows.
All inputs are finite; a program needn't handle non-finite values.
Results may differ from a plain program's by a relative error of at most 0.0064.
Values may be sent and summed in bfloat16 or wider, within the bound.
A program may use at most 128 MiB of HBM per device.

v0:
```python
import math
import jax
import jax.numpy as jnp
from jax import lax
from jax.sharding import PartitionSpec as P

CAP = 128
CLIP_RMS = 0.2


def slots_of(route_block, experts):
    flat_routes = route_block.reshape(-1)
    onehot = (flat_routes[:, None] == jnp.arange(experts, dtype=jnp.int32)[None, :]).astype(
        jnp.int32
    )
    before = jnp.cumsum(onehot, axis=0) - onehot
    position = jnp.sum(before * onehot, axis=1)
    counts = jnp.sum(onehot, axis=0)
    return (flat_routes * CAP + position, counts)


def fill_rows(token_block, cot_block, gate_block, slot_index, counts, experts):
    routed = slot_index.shape[0]
    row_of_slot = (
        jnp.zeros((experts * CAP,), jnp.int32)
        .at[slot_index]
        .set(jnp.arange(routed, dtype=jnp.int32))
    )
    live_slot = (jnp.arange(CAP, dtype=jnp.int32)[None, :] < counts[:, None]).reshape(-1)
    token_of_slot = row_of_slot // 2
    input_rows = jnp.where(
        live_slot[:, None], token_block[token_of_slot], jnp.zeros((), token_block.dtype)
    )
    scaled = gate_block.reshape(-1)[row_of_slot].astype(jnp.float32)[:, None] * cot_block[
        token_of_slot
    ].astype(jnp.float32)
    weighted_rows = jnp.where(live_slot[:, None], scaled, jnp.zeros((), scaled.dtype)).astype(
        jnp.bfloat16
    )
    model_width = token_block.shape[1]
    return (
        input_rows.reshape(experts, CAP, model_width),
        weighted_rows.reshape(experts, CAP, model_width),
    )


def row_contract(left, right):
    return lax.dot_general(
        left, right, (((0,), (0,)), ((), ())), preferred_element_type=jnp.float32
    )


def unit_contract(left, right):
    return lax.dot_general(
        left, right, (((1,), (1,)), ((), ())), preferred_element_type=jnp.float32
    )


def expert_pass(input_rows, weighted_rows, gate_matrix, up_matrix, down_matrix):
    pre_gate = jnp.dot(input_rows, gate_matrix, preferred_element_type=jnp.float32)
    pre_up = jnp.dot(input_rows, up_matrix, preferred_element_type=jnp.float32)
    sigmoid_gate = jax.nn.sigmoid(pre_gate)
    activated = pre_gate * sigmoid_gate
    hidden = (activated * pre_up).astype(jnp.bfloat16)
    grad_hidden = jnp.dot(weighted_rows, down_matrix, preferred_element_type=jnp.float32)
    grad_gate = (
        grad_hidden * pre_up * sigmoid_gate * (1.0 + pre_gate * (1.0 - sigmoid_gate))
    ).astype(jnp.bfloat16)
    grad_up = (grad_hidden * activated).astype(jnp.bfloat16)
    stacked = jnp.stack(
        [
            row_contract(input_rows, grad_gate),
            row_contract(input_rows, grad_up),
            row_contract(weighted_rows, hidden),
        ]
    )
    return (stacked, grad_gate, grad_up)


def per_device(tokens, cotangent, routes, gate_values, gate_weight, up_weight, down_weight):
    experts = lax.axis_size("expert")
    shards = lax.axis_size("dp")
    model_width = tokens.shape[1]
    gate_matrix = gate_weight[0]
    up_matrix = up_weight[0]
    down_matrix = down_weight[0]
    units = gate_matrix.shape[1]
    slot_index, counts = slots_of(routes, experts)
    input_send, weighted_send = fill_rows(
        tokens, cotangent, gate_values, slot_index, counts, experts
    )
    input_recv, weighted_recv, counts_recv = (
        lax.all_to_all(input_send, "expert", split_axis=0, concat_axis=0, tiled=True),
        lax.all_to_all(weighted_send, "expert", split_axis=0, concat_axis=0, tiled=True),
        lax.all_to_all(counts, "expert", split_axis=0, concat_axis=0, tiled=True),
    )
    slot_total = experts * CAP
    input_rows = input_recv.reshape(slot_total, model_width)
    weighted_rows = weighted_recv.reshape(slot_total, model_width)
    grad_sum, grad_gate, grad_up = expert_pass(
        input_rows, weighted_rows, gate_matrix, up_matrix, down_matrix
    )
    summed = lax.psum_scatter(
        unit_contract(gate_matrix, grad_gate) + unit_contract(up_matrix, grad_up),
        "dp",
        scatter_dimension=0,
        tiled=True,
    )
    returned_rows = lax.all_to_all(summed, "expert", split_axis=1, concat_axis=1, tiled=True)
    picked = returned_rows[:, slot_index]
    d_tokens = jnp.sum(picked.reshape(picked.shape[0], slot_index.shape[0] // 2, 2), axis=2).astype(
        jnp.bfloat16
    )
    gradients = grad_sum.astype(jnp.bfloat16)
    owned_rows = lax.all_to_all(gradients, "dp", split_axis=1, concat_axis=2, tiled=True)
    squares = lax.psum(jnp.sum(jnp.square(owned_rows.astype(jnp.float32))), ("dp", "expert"))
    clip_limit = CLIP_RMS * math.sqrt(3.0 * experts * model_width * units * shards)
    clip_scale = clip_limit / jnp.maximum(jnp.sqrt(squares), clip_limit)
    clipped = (owned_rows.astype(jnp.float32) * clip_scale).astype(jnp.bfloat16)
    return (clipped[None], d_tokens)


def solution(mesh):
    return jax.shard_map(
        per_device,
        mesh=mesh,
        in_specs=(
            P("expert", None),
            P("expert", None),
            P("expert", None),
            P("expert", None),
            P("expert", None, "dp"),
            P("expert", None, "dp"),
            P("expert", None, "dp"),
        ),
        out_specs=(P("expert", None, "dp", None), P("dp", "expert")),
        check_vma=False,
    )
```

profile of v0, /device:TPU:1, one launch (start us, length us, event | category | flops | bytes accessed | tf_op | source)
XLA Modules:
  0.0 574.3 jit_solution(8340505373630688563)
XLA Ops:
  13.5 13.8 %gather_fusion = bf16[1024,3072]{1,0:T(8,128)(2,1)} fusion(bf16[256,3072]{1,0:T(8,128)(2,1)} %param.7, s32[1024]{0:T(1024)S(1)} %get-tuple-element.9), kind=kCustom, calls=%fused_computation | custom fusion | bytes 12587008 | tf_op jit(solution)/shard_map/gather | solution.py:32
  27.3 5.9 %broadcast_select_fusion = bf16[8,128,3072]{2,1,0:T(8,128)(2,1)} fusion(bf16[8,128,3072]{2,1,0:T(8,128)(2,1)} %bitcast.59, pred[8,128]{1,0:T(8,128)(4,1)S(1)} %iota_compare_fusion.2), kind=kLoop, calls=%fused_computation.13 | loop fusion | flops 3145728 | bytes 12583936 | tf_op jit(solution)/shard_map/jit(_where)/select_n | solution.py:31
  33.2 8.0 %all-to-all-start = ((bf16[8,128,3072]{2,1,0:T(8,128)(2,1)}), bf16[8,128,3072]{2,1,0:T(8,128)(2,1)}, u32[]{:S(2)}, u32[]{:S(2)}) async-start(bf16[8,128,3072]{2,1,0:T(8,128)(2,1)} %broadcast_select_fusion), calls=%async_computation | async-start | bytes 12582912 | tf_op jit(solution)/shard_map/all_to_all | solution.py:93
  41.3 6.8 %gather_fusion.2 = bf16[1024,3072]{1,0:T(8,128)(2,1)} fusion(bf16[256,3072]{1,0:T(8,128)(2,1)S(1)} %copy-done.2, s32[1024]{0:T(1024)S(1)} %get-tuple-element.9), kind=kCustom, calls=%fused_computation.2 | custom fusion | bytes 12587008 | tf_op jit(solution)/shard_map/gather | solution.py:34
  48.4 6.8 %gather_fusion.1 = bf16[1024]{0:T(1024)(128)(2,1)S(1)} fusion(bf16[512]{0:T(512)(128)(2,1)S(1)} %reshape.131, s32[1024]{0:T(1024)S(1)} %get-tuple-element.8), kind=kCustom, calls=%fused_computation.1 | custom fusion | bytes 8192 | tf_op jit(solution)/shard_map/gather | solution.py:34
  55.2 8.9 %fusion.3 = bf16[8,128,3072]{2,1,0:T(8,128)(2,1)} fusion(bf16[8,128,3072]{2,1,0:T(8,128)(2,1)} %bitcast.58, f32[8,128]{1,0:T(8,128)S(1)} %bitcast_convert_fusion, pred[8,128]{1,0:T(8,128)(4,1)S(1)} %iota_compare_fusion.2), kind=kLoop, calls=%fused_computation.11 | loop fusion | flops 12582912 | bytes 12588032 | tf_op jit(solution)/shard_map/convert_element_type | solution.py:37
  64.2 48.5 %all-to-all-done = bf16[8,128,3072]{2,1,0:T(8,128)(2,1)} async-done(((bf16[8,128,3072]{2,1,0:T(8,128)(2,1)}), bf16[8,128,3072]{2,1,0:T(8,128)(2,1)}, u32[]{:S(2)}, u32[]{:S(2)}) %all-to-all-start) | async-done | bytes 6291488 | tf_op jit(solution)/shard_map/all_to_all | solution.py:93
  112.7 5.5 all-to-all-start.1
  118.2 5.5 fusion.12
  123.7 65.8 %all-to-all-done.1 = bf16[8,128,3072]{2,1,0:T(8,128)(2,1)} async-done(((bf16[8,128,3072]{2,1,0:T(8,128)(2,1)}), bf16[8,128,3072]{2,1,0:T(8,128)(2,1)}, u32[]{:S(2)}, u32[]{:S(2)}) %all-to-all-start.1) | async-done | bytes 6291488 | tf_op jit(solution)/shard_map/all_to_all | solution.py:94
  189.6 5.1 fusion.14
  194.7 5.8 %multiply_convert_fusion.2 = (bf16[1024,256]{1,0:T(8,128)(2,1)S(1)}, bf16[1024,256]{1,0:T(8,128)(2,1)S(1)}, f32[1024,256]{1,0:T(8,128)}) fusion(f32[1024,256]{1,0:T(8,128)S(1)} %fusion.14, f32[1024,256]{1,0:T(8,128)S(1)} %copy-done.7, bf16[1024,3072]{1,0:T(8,128)(2,1)} %bitcast.5, bf16[1,3072,256]{2,1,0:T(8,128)(2,1)S(1)} %copy-done), kind=kOutput, calls=%fused_computation.32 | convolution fusion | flops 1614020608 | bytes 12058624 | tf_op jit(solution)/shard_map/dot_general | solution.py:60
  202.3 6.3 %add_bitcast_fusion = f32[3072,1024]{0,1:T(8,128)} fusion(f32[1024,3072]{1,0:T(8,128)S(1)} %fusion.7, bf16[1024,256]{1,0:T(8,128)(2,1)S(1)} %get-tuple-element.7, bf16[1,3072,256]{2,1,0:T(8,128)(2,1)S(1)} %copy-done.5), kind=kOutput, calls=%fused_computation.12 | convolution fusion | flops 1613758464 | bytes 27262976 | tf_op jit(solution)/shard_map/dot_general | solution.py:54
  208.6 12.6 %copy.24 = f32[3072,1024]{1,0:T(8,128)} copy(f32[3072,1024]{0,1:T(8,128)} %add_bitcast_fusion) | data formatting | bytes 25165824
  225.9 4.8 fusion.4
  230.8 5.2 fusion.6
  236.5 23.9 %copy.19 = bf16[3,3072,256]{2,0,1:T(4,128)(2,1)S(1)} copy(bf16[3,3072,256]{2,1,0:T(8,128)(2,1)S(1)} %pad_maximum_fusion) | data formatting | bytes 9437184 | tf_op jit(solution)/shard_map/stack | solution.py:70
  260.4 187.1 %all_to_all.31 = bf16[3,3072,256]{2,0,1:T(4,128)(2,1)S(1)} all-to-all(bf16[3,3072,256]{2,0,1:T(4,128)(2,1)S(1)} %copy.19), channel_id=1, replica_groups=mesh['dp'=32,'expert'=8] {'dp'}, dimensions={1} | all-to-all | bytes 9437184 | tf_op jit(solution)/shard_map/all_to_all | solution.py:115
  450.2 7.1 %fusion = f32[]{:T(128)} fusion(bf16[3,3072,256]{2,0,1:T(4,128)(2,1)S(1)} %all_to_all.31), kind=kLoop, calls=%fused_computation.7 | loop fusion | flops 7077887 | bytes 4718596 | tf_op jit(solution)/shard_map/reduce_sum | solution.py:116
  457.3 74.5 %psum.7 = f32[]{:T(128)} all-reduce(f32[]{:T(128)} %fusion), channel_id=1, replica_groups=mesh['dp'=32,'expert'=8] {'dp','expert'}, use_global_device_ids=true, to_apply=%region_6.7 | all-reduce | flops 1 | bytes 8 | tf_op jit(solution)/shard_map/psum | solution.py:116
  536.6 9.1 %all-to-all-start.3 = ((f32[96,8,128]{2,0,1:T(8,128)}), f32[96,8,128]{2,0,1:T(8,128)S(1)}, u32[]{:S(2)}, u32[]{:S(2)}) async-start(f32[96,8,128]{2,0,1:T(8,128)} %copy.21), calls=%async_computation.3 | async-start | bytes 786432 | tf_op jit(solution)/shard_map/all_to_all | solution.py:109
  545.7 5.5 fusion.1
  551.2 5.6 copy.20
  556.8 8.3 %convert_element_type.84 = bf16[1,3,96,8192]{3,2,1,0:T(8,128)(2,1)} reshape(bf16[3,96,32,256]{3,2,1,0:T(8,128)(2,1)} %copy.20) | data formatting | bytes 9437184 | tf_op jit(solution)/shard_map/convert_element_type | solution.py:119
  (54 shorter events, 22.7 us)
Async XLA Ops:
  7.2 187.5 %copy-start = (bf16[1,3072,256]{2,1,0:T(8,128)(2,1)S(1)}, bf16[1,3072,256]{2,1,0:T(8,128)(2,1)}, u32[]{:S(2)}) copy-start(bf16[1,3072,256]{2,1,0:T(8,128)(2,1)} %param.11) | copy-start | bytes 4718596
  33.2 8.1 %copy-start.2 = (bf16[256,3072]{1,0:T(8,128)(2,1)S(1)}, bf16[256,3072]{1,0:T(8,128)(2,1)}, u32[]{:S(2)}) copy-start(bf16[256,3072]{1,0:T(8,128)(2,1)} %param.8) | copy-start | bytes 4718596
  33.2 79.4 %all-to-all-start = ((bf16[8,128,3072]{2,1,0:T(8,128)(2,1)}), bf16[8,128,3072]{2,1,0:T(8,128)(2,1)}, u32[]{:S(2)}, u32[]{:S(2)}) async-start(bf16[8,128,3072]{2,1,0:T(8,128)(2,1)} %broadcast_select_fusion), calls=%async_computation | async-start | bytes 12582912 | tf_op jit(solution)/shard_map/all_to_all | solution.py:93
  41.3 6.8 %copy-start.6 = (bf16[256,2]{0,1:T(2,128)(2,1)S(1)}, bf16[256,2]{0,1:T(2,128)(2,1)}, u32[]{:S(2)}) copy-start(bf16[256,2]{0,1:T(2,128)(2,1)} %param.10) | copy-start | bytes 3076
  64.2 54.0 %copy-start.4 = (bf16[1,3072,256]{2,1,0:T(8,128)(2,1)S(1)}, bf16[1,3072,256]{2,1,0:T(8,128)(2,1)}, u32[]{:S(2)}) copy-start(bf16[1,3072,256]{2,1,0:T(8,128)(2,1)} %param.12) | copy-start | bytes 4718596
  112.7 76.9 %all-to-all-start.1 = ((bf16[8,128,3072]{2,1,0:T(8,128)(2,1)}), bf16[8,128,3072]{2,1,0:T(8,128)(2,1)}, u32[]{:S(2)}, u32[]{:S(2)}) async-start(bf16[8,128,3072]{2,1,0:T(8,128)(2,1)} %fusion.3), calls=%async_computation.1 | async-start | bytes 12582912 | tf_op jit(solution)/shard_map/all_to_all | solution.py:94
  118.2 416.3 %reduce-scatter.4.cloned.1.call-start = ((), (), s32[]{:S(2)}) async-start(), calls=%async_computation.5 | async-start | bytes 12976128
  189.6 5.1 copy-start.7
  200.5 1.8 copy-start.5
  225.9 4.8 copy-start.8
  225.9 4.8 copy-start.9
  447.6 2.6 copy-start.3
  536.6 28.5 %all-to-all-start.3 = ((f32[96,8,128]{2,0,1:T(8,128)}), f32[96,8,128]{2,0,1:T(8,128)S(1)}, u32[]{:S(2)}, u32[]{:S(2)}) async-start(f32[96,8,128]{2,0,1:T(8,128)} %copy.21), calls=%async_computation.3 | async-start | bytes 786432 | tf_op jit(solution)/shard_map/all_to_all | solution.py:109
  551.2 16.3 %copy-start.1 = (bf16[1,3072,256]{2,1,0:T(8,128)(2,1)S(1)}, bf16[1,3072,256]{2,1,0:T(8,128)(2,1)}, u32[]{:S(2)}) copy-start(bf16[1,3072,256]{2,1,0:T(8,128)(2,1)} %param.11) | copy-start | bytes 4718596
Sparse Core Ops, SparseCore 0:
  221.3 313.0 reduce-scatter.3
where the time goes:
time: 575 us; the launch traced here: 574 us
  blocking collectives  262 us (46%)
  waiting for transfers between devices  116 us (20%)
  local copies, waits for them, and re-layouts  88.9 us (15%)
  matrix products  39.2 us (7%)
  other arithmetic  30.7 us (5%)
  starting transfers between devices  22.6 us (4%)
  between operations  15 us (3%)
    all_to_all x1, blocking collectives, per_device(): lax.all_to_all(gradients, 'dp', split_axis=1, concat_axis=2, tiled=True)  187 us
    psum x1, blocking collectives, per_device(): lax.psum(jnp.sum(jnp.square(owned_rows.astype(jnp.float32))), ('dp', 'exp...  74.5 us
    all_to_all x1, waiting for transfers between devices, per_device(): lax.all_to_all(weighted_send, 'expert', split_axis=0, concat_axis=0, tile...  65.8 us
    all_to_all x1, waiting for transfers between devices, per_device(): lax.all_to_all(input_send, 'expert', split_axis=0, concat_axis=0, tiled=T...  48.5 us
    another operation x1, local copies, waits for them, and re-layouts, expert_pass(): jnp.stack([row_contract(input_rows, grad_gate), row_contract(input_rows,...  23.9 us
    unnamed x25, local copies, waits for them, and re-layouts  18.1 us
    dot_general x3, matrix products, row_contract(): lax.dot_general(left, right, (((0,), (0,)), ((), ())), preferred_element_...  14.7 us
    convert_element_type x2, local copies, waits for them, and re-layouts, per_device(): clipped = (owned_rows.astype(jnp.float32) * clip_scale).astype(jnp.bfloat16)  13.9 us
  transfers between devices with their start and end apart: 4, of which 3 were waited for; matrix products, arithmetic and copies ran while one was open for 16% of the time, Pallas kernels for 0%

commit v1 on v0

--- a/solution.py
+++ b/solution.py
@@ -6,6 +6,13 @@
 
 CAP = 128
 CLIP_RMS = 0.2
+
+
+def trade_parts(block, axis, split, join):
+    count = lax.axis_size(axis)
+    blocks = jnp.stack(jnp.split(block, count, axis=split), axis=0)
+    blocks = lax.all_to_all(blocks, axis, split_axis=0, concat_axis=0)
+    return jnp.concatenate(blocks, axis=join)
 
 
 def slots_of(route_block, experts):
@@ -112,7 +119,7 @@
         jnp.bfloat16
     )
     gradients = grad_sum.astype(jnp.bfloat16)
-    owned_rows = lax.all_to_all(gradients, "dp", split_axis=1, concat_axis=2, tiled=True)
+    owned_rows = trade_parts(gradients, "dp", 1, 2)
     squares = lax.psum(jnp.sum(jnp.square(owned_rows.astype(jnp.float32))), ("dp", "expert"))
     clip_limit = CLIP_RMS * math.sqrt(3.0 * experts * model_width * units * shards)
     clip_scale = clip_limit / jnp.maximum(jnp.sqrt(squares), clip_limit)

time: 575 us -> 565 us (0.983)
  waiting for transfers between devices: 116 us -> 175 us
  blocking collectives: 262 us -> 228 us
  local copies, waits for them, and re-layouts: 88.9 us -> 58.1 us
  other arithmetic: 30.7 us -> 24.4 us
    unnamed x2, waiting for transfers between devices: 1.92 us -> 51.2 us
    all_to_all x1, blocking collectives: 187 us -> 153 us  [trade_parts(): blocks = lax.all_to_all(blocks, axis, split_axis=0, concat_axis=0)]
    another operation x2, local copies, waits for them, and re-layouts: 23.9 us -> 0.02 us  [the longest x1 0.01 us: trade_parts(): blocks = jnp.stack(jnp.split(block, count, axis=split), axis=0)]
    all_to_all x1, waiting for transfers between devices: 48.5 us -> 65.3 us  [per_device(): lax.all_to_all(input_send, 'expert', split_axis=0, concat_axis=0, tiled=T...]
    all_to_all x1, waiting for transfers between devices: 65.8 us -> 58.6 us  [per_device(): lax.all_to_all(weighted_send, 'expert', split_axis=0, concat_axis=0, tile...]
    gather x1, local copies, waits for them, and re-layouts: 13.8 us -> 6.83 us  [fill_rows(): token_block[token_of_slot]]
    unnamed x25 -> x58, local copies, waits for them, and re-layouts: 18.1 us -> 18.9 us
  transfers between devices with their start and end apart: 4 -> 4, of which waited for: 3 -> 3; matrix products, arithmetic and copies ran while one was open for 16% -> 10% of each run, Pallas kernels for 0% -> 0%
where the time goes in v1:
time: 565 us; the launch traced here: 564 us
  blocking collectives  228 us (40%)
  waiting for transfers between devices  175 us (31%)
  local copies, waits for them, and re-layouts  58.1 us (10%)
  matrix products  39.7 us (7%)
  other arithmetic  24.4 us (4%)
  starting transfers between devices  22.8 us (4%)
  between operations  15.3 us (3%)
    all_to_all x1, blocking collectives, trade_parts(): blocks = lax.all_to_all(blocks, axis, split_axis=0, concat_axis=0)  153 us
    psum x1, blocking collectives, per_device(): lax.psum(jnp.sum(jnp.square(owned_rows.astype(jnp.float32))), ('dp', 'exp...  75.7 us
    all_to_all x1, waiting for transfers between devices, per_device(): lax.all_to_all(input_send, 'expert', split_axis=0, concat_axis=0, tiled=T...  65.3 us
    all_to_all x1, waiting for transfers between devices, per_device(): lax.all_to_all(weighted_send, 'expert', split_axis=0, concat_axis=0, tile...  58.6 us
    unnamed x2, waiting for transfers between devices  51.2 us
    unnamed x58, local copies, waits for them, and re-layouts  18.9 us
    dot_general x3, matrix products, row_contract(): lax.dot_general(left, right, (((0,), (0,)), ((), ())), preferred_element_...  14.6 us
    convert_element_type x2, local copies, waits for them, and re-layouts, per_device(): clipped = (owned_rows.astype(jnp.float32) * clip_scale).astype(jnp.bfloat16)  13.2 us
  transfers between devices with their start and end apart: 4, of which 3 were waited for; matrix products, arithmetic and copies ran while one was open for 10% of the time, Pallas kernels for 0%

profile of v1, /device:TPU:1, one launch (start us, length us, event | category | flops | bytes accessed | tf_op | source)
XLA Modules:
  0.0 563.6 jit_solution(6231794232357759737)
XLA Ops:
  14.4 6.8 %gather_fusion.1 = bf16[1024]{0:T(1024)(128)(2,1)S(1)} fusion(bf16[512]{0:T(512)(128)(2,1)S(1)} %reshape.127, s32[1024]{0:T(1024)S(1)} %get-tuple-element.8), kind=kCustom, calls=%fused_computation.1 | custom fusion | bytes 8192 | tf_op jit(solution)/shard_map/gather | solution.py:41
  21.3 6.8 %gather_fusion.2 = bf16[1024,3072]{1,0:T(8,128)(2,1)} fusion(bf16[256,3072]{1,0:T(8,128)(2,1)S(1)} %copy-done.2, s32[1024]{0:T(1024)S(1)} %get-tuple-element.9), kind=kCustom, calls=%fused_computation.2 | custom fusion | bytes 12587008 | tf_op jit(solution)/shard_map/gather | solution.py:41
  28.2 8.9 %fusion.1 = bf16[8,128,3072]{2,1,0:T(8,128)(2,1)} fusion(bf16[8,128,3072]{2,1,0:T(8,128)(2,1)} %bitcast.186, f32[8,128]{1,0:T(8,128)S(1)} %bitcast_convert_fusion, pred[8,128]{1,0:T(8,128)(4,1)S(1)} %iota_compare_fusion.2), kind=kLoop, calls=%fused_computation.7 | loop fusion | flops 12582912 | bytes 12588032 | tf_op jit(solution)/shard_map/convert_element_type | solution.py:44
  37.1 8.0 %all-to-all-start.1 = ((bf16[8,128,3072]{2,1,0:T(8,128)(2,1)}), bf16[8,128,3072]{2,1,0:T(8,128)(2,1)}, u32[]{:S(2)}, u32[]{:S(2)}) async-start(bf16[8,128,3072]{2,1,0:T(8,128)(2,1)} %fusion.1), calls=%async_computation.1 | async-start | bytes 12582912 | tf_op jit(solution)/shard_map/all_to_all | solution.py:101
  45.2 6.8 %gather_fusion = bf16[1024,3072]{1,0:T(8,128)(2,1)} fusion(bf16[256,3072]{1,0:T(8,128)(2,1)S(1)} %copy-done.3, s32[1024]{0:T(1024)S(1)} %get-tuple-element.9), kind=kCustom, calls=%fused_computation | custom fusion | bytes 12587008 | tf_op jit(solution)/shard_map/gather | solution.py:39
  52.0 5.9 %broadcast_select_fusion = bf16[8,128,3072]{2,1,0:T(8,128)(2,1)} fusion(bf16[8,128,3072]{2,1,0:T(8,128)(2,1)} %bitcast.185, pred[8,128]{1,0:T(8,128)(4,1)S(1)} %iota_compare_fusion.2), kind=kLoop, calls=%fused_computation.13 | loop fusion | flops 3145728 | bytes 12583936 | tf_op jit(solution)/shard_map/jit(_where)/select_n | solution.py:38
  57.9 58.6 %all-to-all-done.1 = bf16[8,128,3072]{2,1,0:T(8,128)(2,1)} async-done(((bf16[8,128,3072]{2,1,0:T(8,128)(2,1)}), bf16[8,128,3072]{2,1,0:T(8,128)(2,1)}, u32[]{:S(2)}, u32[]{:S(2)}) %all-to-all-start.1) | async-done | bytes 6291488 | tf_op jit(solution)/shard_map/all_to_all | solution.py:101
  116.6 5.5 all-to-all-start
  122.1 6.1 %fusion.15 = f32[1024,256]{1,0:T(8,128)} fusion(bf16[1024,3072]{1,0:T(8,128)(2,1)} %bitcast.8, bf16[1,3072,256]{2,1,0:T(8,128)(2,1)} %param.13), kind=kOutput, calls=%fused_computation.29 | convolution fusion | flops 1610612736 | bytes 8912896 | tf_op jit(solution)/shard_map/dot_general | solution.py:72
  128.2 65.3 %all-to-all-done = bf16[8,128,3072]{2,1,0:T(8,128)(2,1)} async-done(((bf16[8,128,3072]{2,1,0:T(8,128)(2,1)}), bf16[8,128,3072]{2,1,0:T(8,128)(2,1)}, u32[]{:S(2)}, u32[]{:S(2)}) %all-to-all-start) | async-done | bytes 6291488 | tf_op jit(solution)/shard_map/all_to_all | solution.py:100
  193.5 4.7 fusion.13
  198.2 6.2 %multiply_convert_fusion.2 = (bf16[1024,256]{1,0:T(8,128)(2,1)S(1)}, bf16[1024,256]{1,0:T(8,128)(2,1)S(1)}, f32[1024,256]{1,0:T(8,128)}) fusion(f32[1024,256]{1,0:T(8,128)S(1)} %copy-done.9, f32[1024,256]{1,0:T(8,128)S(1)} %fusion.13, bf16[1024,3072]{1,0:T(8,128)(2,1)} %bitcast.5, bf16[1,3072,256]{2,1,0:T(8,128)(2,1)S(1)} %copy-done), kind=kOutput, calls=%fused_computation.33 | convolution fusion | flops 1614020608 | bytes 12058624 | tf_op jit(solution)/shard_map/dot_general | solution.py:67
  206.2 6.3 %add_bitcast_fusion = f32[3072,1024]{0,1:T(8,128)} fusion(f32[1024,3072]{1,0:T(8,128)S(1)} %fusion.8, bf16[1024,256]{1,0:T(8,128)(2,1)S(1)} %get-tuple-element.7, bf16[1,3072,256]{2,1,0:T(8,128)(2,1)S(1)} %copy-done.6), kind=kOutput, calls=%fused_computation.8 | convolution fusion | flops 1613758464 | bytes 27262976 | tf_op jit(solution)/shard_map/dot_general | solution.py:61
  212.5 12.6 %copy.22 = f32[3072,1024]{1,0:T(8,128)} copy(f32[3072,1024]{0,1:T(8,128)} %add_bitcast_fusion) | data formatting | bytes 25165824
  225.1 4.7 fusion.5
  229.8 4.8 fusion.6
  234.6 5.1 fusion.7
  241.0 152.6 %all_to_all.27 = bf16[32,3,96,256]{3,2,1,0:T(8,128)(2,1)S(1)} all-to-all(bf16[32,3,96,256]{3,2,1,0:T(8,128)(2,1)S(1)} %fusion.19), channel_id=1, replica_groups=mesh['dp'=32,'expert'=8] {'dp'}, dimensions={0} | all-to-all | bytes 9437184 | tf_op jit(solution)/shard_map/all_to_all | solution.py:14
  398.8 75.7 %psum.7 = f32[]{:T(128)} all-reduce(f32[]{:T(128)} %fusion.2), channel_id=1, replica_groups=mesh['dp'=32,'expert'=8] {'dp','expert'}, use_global_device_ids=true, to_apply=%region_6.7 | all-reduce | flops 1 | bytes 8 | tf_op jit(solution)/shard_map/psum | solution.py:123
  475.2 51.2 %reduce-scatter.4.cloned.1.call-done = f32[96,1024]{1,0:T(8,128)} async-done(((f32[3072,1024]{1,0:T(8,128)}), f32[96,1024]{1,0:T(8,128)}) %reduce-scatter.4.cloned.1.call-update) | async-done | bytes 393232
  528.6 9.2 %all-to-all-start.3 = ((f32[96,8,128]{2,0,1:T(8,128)}), f32[96,8,128]{2,0,1:T(8,128)S(1)}, u32[]{:S(2)}, u32[]{:S(2)}) async-start(f32[96,8,128]{2,0,1:T(8,128)} %copy.19), calls=%async_computation.3 | async-start | bytes 786432 | tf_op jit(solution)/shard_map/all_to_all | solution.py:116
  537.8 3.5 fusion.4
  541.3 4.9 copy.18
  546.2 8.3 %convert_element_type.85 = bf16[1,3,96,8192]{3,2,1,0:T(8,128)(2,1)} reshape(bf16[3,96,32,256]{3,2,1,0:T(8,128)(2,1)} %copy.18) | data formatting | bytes 9437184 | tf_op jit(solution)/shard_map/convert_element_type | solution.py:126
  (87 shorter events, 19.8 us)
Async XLA Ops:
  7.2 191.0 %copy-start = (bf16[1,3072,256]{2,1,0:T(8,128)(2,1)S(1)}, bf16[1,3072,256]{2,1,0:T(8,128)(2,1)}, u32[]{:S(2)}) copy-start(bf16[1,3072,256]{2,1,0:T(8,128)(2,1)} %param.11) | copy-start | bytes 4718596
  7.2 14.2 %copy-start.2 = (bf16[256,3072]{1,0:T(8,128)(2,1)S(1)}, bf16[256,3072]{1,0:T(8,128)(2,1)}, u32[]{:S(2)}) copy-start(bf16[256,3072]{1,0:T(8,128)(2,1)} %param.8) | copy-start | bytes 4718596
  37.1 8.1 %copy-start.3 = (bf16[256,3072]{1,0:T(8,128)(2,1)S(1)}, bf16[256,3072]{1,0:T(8,128)(2,1)}, u32[]{:S(2)}) copy-start(bf16[256,3072]{1,0:T(8,128)(2,1)} %param.7) | copy-start | bytes 4718596
  37.1 79.4 %all-to-all-start.1 = ((bf16[8,128,3072]{2,1,0:T(8,128)(2,1)}), bf16[8,128,3072]{2,1,0:T(8,128)(2,1)}, u32[]{:S(2)}, u32[]{:S(2)}) async-start(bf16[8,128,3072]{2,1,0:T(8,128)(2,1)} %fusion.1), calls=%async_computation.1 | async-start | bytes 12582912 | tf_op jit(solution)/shard_map/all_to_all | solution.py:101
  116.6 76.9 %all-to-all-start = ((bf16[8,128,3072]{2,1,0:T(8,128)(2,1)}), bf16[8,128,3072]{2,1,0:T(8,128)(2,1)}, u32[]{:S(2)}, u32[]{:S(2)}) async-start(bf16[8,128,3072]{2,1,0:T(8,128)(2,1)} %broadcast_select_fusion), calls=%async_computation | async-start | bytes 12582912 | tf_op jit(solution)/shard_map/all_to_all | solution.py:100
  122.1 404.4 %reduce-scatter.4.cloned.1.call-start = ((), (), s32[]{:S(2)}) async-start(), calls=%async_computation.5 | async-start | bytes 12976128
  122.1 71.4 %copy-start.5 = (bf16[1,3072,256]{2,1,0:T(8,128)(2,1)S(1)}, bf16[1,3072,256]{2,1,0:T(8,128)(2,1)}, u32[]{:S(2)}) copy-start(bf16[1,3072,256]{2,1,0:T(8,128)(2,1)} %param.12) | copy-start | bytes 4718596
  193.5 4.7 copy-start.9
  198.1 6.2 %copy-start.7 = (f32[1024,256]{1,0:T(8,128)}, f32[1024,256]{1,0:T(8,128)S(1)}, u32[]{:S(2)}) copy-start(f32[1024,256]{1,0:T(8,128)S(1)} %fusion.13) | copy-start | bytes 3145732
  204.3 1.8 copy-start.6
  229.7 4.8 copy-start.8
  229.8 4.8 copy-start.10
  393.6 2.2 copy-start.4
  528.6 25.9 %all-to-all-start.3 = ((f32[96,8,128]{2,0,1:T(8,128)}), f32[96,8,128]{2,0,1:T(8,128)S(1)}, u32[]{:S(2)}, u32[]{:S(2)}) async-start(f32[96,8,128]{2,0,1:T(8,128)} %copy.19), calls=%async_computation.3 | async-start | bytes 786432 | tf_op jit(solution)/shard_map/all_to_all | solution.py:116
  541.3 15.5 %copy-start.1 = (bf16[1,3072,256]{2,1,0:T(8,128)(2,1)S(1)}, bf16[1,3072,256]{2,1,0:T(8,128)(2,1)}, u32[]{:S(2)}) copy-start(bf16[1,3072,256]{2,1,0:T(8,128)(2,1)} %param.11) | copy-start | bytes 4718596
Sparse Core Ops, SparseCore 0:
  225.2 301.1 reduce-scatter.3
